TPU v7x, 32 devices: a whole 2x2x4 slice. The times are simulated.
32 devices in a mesh: sweep: 4 (over y, x), azim: 8 (over z, core).
Axes of the slice: x: 2, y: 2, z: 4, core: 2. Of those that a mesh axis runs over, the one named last changes fastest.
Arguments:
- latents: bfloat16 [8, 8, 256, 512], P('sweep', None, 'azim'), may hold values from -6 to 6
- cotangent: bfloat16 [8, 8, 256, 512], P('sweep', None, 'azim'), may hold values from -6 to 6
- conv_kernel: float32 [9, 512], replicated, may hold values from -2 to 2
- conv_bias: float32 [512], replicated, may hold values from -3 to 3
- norm_gain: float32 [512], replicated, may hold values from 0.25 to 1.75
- w_query: bfloat16 [512, 256], replicated, may hold values from -2 to 2
- w_key: bfloat16 [512, 256], replicated, may hold values from -2 to 2
- w_value: bfloat16 [512, 256], replicated, may hold values from -0.25 to 0.25
- w_output: bfloat16 [512, 256], replicated, may hold values from -0.375 to 0.375
Outputs:
- grad_latents: float32 [8, 8, 256, 512], P('sweep', None, 'azim')
- grad_kernel: float32 [9, 512], replicated
- grad_bias: float32 [512], replicated
- grad_gain: float32 [512], replicated
- grad_query: float32 [512, 256], P('azim')
- grad_key: float32 [512, 256], P('azim')
- grad_value: float32 [512, 256], P('azim')
- grad_output: float32 [512, 256], P('azim')
All inputs are finite; a program needn't handle non-finite values.
Results may differ from a plain program's by a relative error of at most 0.01.
The roundings to bfloat16 on the way count: a program that leaves them out, or rounds other values in their place, can miss the bound.
Values may be sent and summed in bfloat16 or wider, within the bound.
A program may use at most 64 MiB of HBM per device.

v0:
```python
import functools
import math

import jax
import jax.numpy as jnp
from jax import lax
from jax.experimental import pallas as pl
from jax.experimental.pallas import tpu as pltpu
from jax.sharding import PartitionSpec as P

DH = 64
EPS = 1e-06
LANES = 128
PIX = 16
MESH = pl.DeviceIdType.MESH
VMEM = pl.BlockSpec(memory_space=pltpu.VMEM)
ANY = pl.BlockSpec(memory_space=pl.ANY)
BIG = 56 * 1024 * 1024


def remote(src, dst, send, recv, where):
    return pltpu.make_async_remote_copy(
        src_ref=src, dst_ref=dst, send_sem=send, recv_sem=recv, device_id=where, device_id_type=MESH
    )


def greet(partners):
    barrier = pltpu.get_barrier_semaphore()
    for where in partners:
        pl.semaphore_signal(barrier, inc=1, device_id=where, device_id_type=MESH)
    pl.semaphore_wait(barrier, len(partners))


def store_shifted(dst, s, h, val):
    width = val.shape[0]
    dst[1, s, h + 1] = val
    dst[0, s, h + 1] = pltpu.roll(val, 1, 0)
    dst[2, s, h + 1] = pltpu.roll(val, width - 1, 0)


def patch_edges(dst, left, right, sweeps, height, width):
    for s in range(sweeps):
        for h in range(height):
            i = s * height + h
            dst[0, s, h + 1, 0:1, :] = left[i : i + 1, :]
            dst[2, s, h + 1, width - 1 : width, :] = right[i : i + 1, :]


def zero_frame(dst, sweeps, height):
    for b in range(3):
        for s in range(sweeps):
            dst[b, s, 0] = jnp.zeros(dst.shape[3:], jnp.float32)
            dst[b, s, height + 1] = jnp.zeros(dst.shape[3:], jnp.float32)


def dot(a, b, dims):
    return lax.dot_general(a, b, (dims, ((), ())), preferred_element_type=jnp.float32)


NN = ((1,), (0,))
NT = ((1,), (1,))
TN = ((0,), (0,))


def block_kernel(
    groups, strips, heads, predivide,
    lat, cot, kern, bias, gain_ref, wq_hbm, wk_hbm, wv_hbm, wo_hbm,
    out_lat, out_fin, out_small,
    act, gy, y_src, y_pix, cot_pix, grad, ret,
    fore_left, fore_right, fore_in_left, fore_in_right, edge_left, edge_right, in_left, in_right,
    weights, left_s, right_s, grad_att_s, mats, pair_buf, acc, sweep_buf, acc2, z_buf, early_z, early_sum, late_buf, lat_out,
    taps, small, small_pair, small_sweep, small_z,
    w_sem, own_sem, a2a_send, a2a_recv, back_send, back_recv, halo_send, halo_recv,
    pair_send, pair_recv, sweep_send, sweep_recv, z_send, z_recv, fin_send, fin_recv,
    sp_send, sp_recv, ss_send, ss_recv, sz_send, sz_recv, lat_sem, ez_send, ez_recv, late_send, late_recv,
):
    sweeps, height, width, channels = lat.shape
    each = height * width // groups
    planes = strips // 2
    inner = right_s.shape[2]
    me = lax.axis_index("sweep")
    az = lax.axis_index("azim")
    core = lax.rem(az, 2)
    z = az // 2
    other = az + 1 - 2 * core
    right, left = lax.rem(az + 1, strips), lax.rem(az + strips - 1, strips)
    partners = [lax.rem(me + k, groups) for k in range(1, groups)]
    z_partners = [lax.rem(z + k, planes) for k in range(1, planes)]
    pending = []

    def send(*args):
        copy = remote(*args)
        copy.start()
        pending.append(copy)
        return copy

    loads = []
    for i, w in enumerate((wq_hbm, wk_hbm, wv_hbm, wo_hbm)):
        loads.append(pltpu.make_async_copy(w, weights.at[i], w_sem.at[i]))
        loads[-1].start()
    greet(
        [{"sweep": g} for g in partners]
        + [{"azim": left}, {"azim": right}, {"azim": other}]
        + [{"azim": p * 2 + core} for p in z_partners]
    )
    mine = pl.ds(pl.multiple_of(me * each, PIX), each)
    slots = pl.ds(me * sweeps, sweeps)

    for s in range(sweeps):
        for h in range(height):
            i = s * height + h
            fore_left[i : i + 1, :] = lat[s, h, 0:16, :].astype(jnp.float32)[0:1]
            fore_right[i : i + 1, :] = lat[s, h, width - 16 : width, :].astype(jnp.float32)[15:16]
    to_right = send(fore_right, fore_in_left, halo_send.at[0], halo_recv.at[0], {"azim": right})
    to_left = send(fore_left, fore_in_right, halo_send.at[1], halo_recv.at[1], {"azim": left})

    def give(k, g, source, target, stage, count, send_sem, recv_sem):
        there = pl.ds(pl.multiple_of(g * each + stage * count, PIX), count)
        here = slice(stage * count, (stage + 1) * count)
        return send(source.at[:, there, :], target.at[slots, here, :], send_sem, recv_sem, {"sweep": g})

    cot_copies = [give(k, g, cot, cot_pix, 0, each, a2a_send.at[0, k], a2a_recv.at[0, k]) for k, g in enumerate(partners)]
    cot_own = pltpu.make_async_copy(cot.at[:, mine, :], cot_pix.at[slots], own_sem.at[0])
    cot_own.start()

    for s in range(sweeps):
        def activate(h, carry, s=s):
            x = lat[s, h].astype(jnp.float32)
            store_shifted(act, s, h, x / (1.0 + jnp.exp(-x)))
            return carry
        lax.fori_loop(0, height, activate, 0)
    zero_frame(act, sweeps, height)
    zero_frame(gy, sweeps, height)
    taps[...] = jnp.zeros(taps.shape, jnp.float32)
    to_right.wait_recv()
    to_left.wait_recv()
    for ref in (fore_in_left, fore_in_right):
        x = ref[...]
        ref[...] = x / (1.0 + jnp.exp(-x))
    patch_edges(act, fore_in_left, fore_in_right, sweeps, height, width)

    def convolve_row(s, h):
        total = lat[s, h].astype(jnp.float32) + bias[...]
        for a in range(3):
            for b in range(3):
                total = total + kern[3 * a + b : 3 * a + b + 1, :] * act[b, s, h + a]
        y_src[s, pl.ds(pl.multiple_of(h * width, PIX), width), :] = total.astype(jnp.bfloat16)

    lines = height // groups if groups <= height else 1
    count = each // lines
    y_copies = [[] for _ in range(lines)]

    def give_y(k, g, stage):
        y_copies[stage].append(
            give(k, g, y_src, y_pix, stage, count, a2a_send.at[1 + stage, k], a2a_recv.at[1 + stage, k])
        )

    if groups <= height:
        for stage in range(lines):
            for k, g in enumerate(partners + [me]):
                for sweep in range(sweeps):
                    convolve_row(sweep, g * lines + stage)
                if k < groups - 1:
                    give_y(k, g, stage)
    else:
        def whole(i, carry):
            convolve_row(i // height, i % height)
            return carry
        lax.fori_loop(0, sweeps * height, whole, 0)
        for k, g in enumerate(partners):
            give_y(k, g, 0)
    y_own = pltpu.make_async_copy(y_src.at[:, mine, :], y_pix.at[slots], own_sem.at[1])
    y_own.start()

    m = groups * sweeps * PIX
    blocks = each // PIX
    total_sweeps = groups * sweeps
    scale = 1.0 / math.sqrt(DH)
    gain = gain_ref[...]
    for load in loads:
        load.wait()
    for copy in cot_copies:
        copy.wait_recv()
    cot_own.wait()
    for block in range(blocks):
        at = slice(block * PIX, (block + 1) * PIX)
        own = slice(block * m, (block + 1) * m)
        rows = cot_pix[:, at, :].reshape(m, channels)
        left_s[1, own, :] = rows
        grad_att_s[own, :] = dot(rows, weights[3], NN).astype(jnp.bfloat16)
    row_pix = lax.broadcasted_iota(jnp.int32, (m, m), 0) % PIX
    col_pix = lax.broadcasted_iota(jnp.int32, (m, m), 1) % PIX
    same = row_pix == col_pix
    same = jnp.concatenate([same] * heads, axis=0)
    lane_head = lax.broadcasted_iota(jnp.int32, (1, inner), 1) // DH

    def spread(value):
        return jnp.concatenate(
            [jnp.where(lane_head == h, value, jnp.zeros_like(value)) for h in range(heads)], axis=0
        )

    def collect(value):
        total = jnp.where(lane_head == 0, value[0:m], 0.0)
        for h in range(1, heads):
            total = jnp.where(lane_head == h, value[h * m : (h + 1) * m], total)
        return total

    y_own.wait()
    back, back_own = [], []
    gain_total = jnp.zeros((1, channels), jnp.float32)
    several = count // PIX
    for stage in range(lines):
        for copy in y_copies[stage]:
            copy.wait_recv()
        base = stage * count
        span = slice(stage * several * m, (stage + 1) * several * m)
        y = jnp.concatenate(
            [
                y_pix[:, base + i * PIX : base + (i + 1) * PIX, :].reshape(m, channels)
                for i in range(several)
            ],
            axis=0,
        ).astype(jnp.float32)
        root = jnp.sqrt(jnp.mean(y * y, axis=-1, keepdims=True) + EPS)
        inverse = 1.0 / root
        normed = (y * inverse * gain).astype(jnp.bfloat16)
        left_s[0, span, :] = normed
        queries = dot(normed, weights[0], NN).astype(jnp.bfloat16)
        keys = dot(normed, weights[1], NN).astype(jnp.bfloat16)
        values = dot(normed, weights[2], NN).astype(jnp.bfloat16)
        grads = []
        for i in range(several):
            part = slice(i * m, (i + 1) * m)
            own = slice((stage * several + i) * m, (stage * several + i + 1) * m)
            key, value = keys[part], values[part]
            query_x = spread(queries[part])
            grad_att_x = spread(grad_att_s[own, :])
            scores = jnp.where(same, dot(query_x, key, NT) * scale, -1e30)
            top = jnp.max(scores, axis=-1, keepdims=True)
            expon = jnp.exp(scores - top)
            probs = expon / jnp.sum(expon, axis=-1, keepdims=True)
            probs_low = probs.astype(jnp.bfloat16)
            right_s[3, own, :] = collect(dot(probs_low, value, NN)).astype(jnp.bfloat16)
            grad_probs = dot(grad_att_x, value, NT)
            inner_sum = jnp.sum(probs * grad_probs, axis=-1, keepdims=True)
            grad_scores = (probs * (grad_probs - inner_sum) * scale).astype(jnp.bfloat16)
            grad_v = dot(probs_low, grad_att_x, TN).astype(jnp.bfloat16)
            grad_q = collect(dot(grad_scores, key, NN)).astype(jnp.bfloat16)
            grad_k = dot(grad_scores, query_x, TN).astype(jnp.bfloat16)
            right_s[0, own, :] = grad_q
            right_s[1, own, :] = grad_k
            right_s[2, own, :] = grad_v
            grads.append((grad_q, grad_k, grad_v))
        grad_q, grad_k, grad_v = (jnp.concatenate(each_grad, axis=0) for each_grad in zip(*grads))
        grad_normed = (
            dot(grad_q, weights[0], NT) + dot(grad_k, weights[1], NT) + dot(grad_v, weights[2], NT)
        )
        gain_total = gain_total + jnp.sum(grad_normed * y * inverse, axis=0, keepdims=True)
        gained = grad_normed * gain
        mean = jnp.mean(gained * y, axis=-1, keepdims=True)
        grad_attn = (inverse * (gained - y * mean * inverse * inverse)).astype(jnp.bfloat16)
        for i in range(several):
            at = slice(base + i * PIX, base + (i + 1) * PIX)
            grad[:, at, :] = grad_attn[i * m : (i + 1) * m].reshape(total_sweeps, PIX, channels)
        at = slice(base, base + count)
        here = pl.ds(pl.multiple_of(me * each + base, PIX), count)
        for k, g in enumerate(partners):
            back.append(
                send(
                    grad.at[pl.ds(g * sweeps, sweeps), at, :], ret.at[:, here, :],
                    back_send.at[stage, k], back_recv.at[stage, k], {"sweep": g},
                )
            )
        back_own.append(
            pltpu.make_async_copy(grad.at[slots, at, :], ret.at[:, here, :], own_sem.at[2 + stage])
        )
        back_own[-1].start()

    _, lanes, _, _, parts, rows, _ = mats.shape
    per = 4 * lanes * parts // groups
    interleave = groups == 4
    order = [lax.rem(me + k + 1, 4) if interleave else k for k in range(4)]
    pairs = []
    for n, i in enumerate(order):
        full = dot(left_s[i // 3], right_s[i], TN)
        for j in range(lanes):
            part = full[:, j * LANES : (j + 1) * LANES]
            mats[i, j] = part.reshape(planes, 2, parts, rows, LANES)
        pairs.append(
            send(mats.at[i, :, :, 1 - core], pair_buf.at[i], pair_send.at[n], pair_recv.at[n], {"azim": other})
        )
    scatter, early = [], []
    units = lanes * parts
    split = rows - rows * 3 // 8 // 8 * 8

    def scatter_to(k, g):
        scatter.append(
            send(acc.at[pl.ds(g * per, per), :, 0:split], sweep_buf.at[k], sweep_send.at[k], sweep_recv.at[k], {"sweep": g})
        )

    for n, i in enumerate(order):
        pairs[n].wait_recv()
        for j in range(lanes):
            for p in range(parts):
                for q in range(planes):
                    acc[(i * lanes + j) * parts + p, q] = mats[i, j, q, core, p] + pair_buf[i, j, q, p]
        if interleave and n < 3:
            scatter_to(n, i)
        if split < rows:
            of = pl.ds(i * units, units)
            for k, p in enumerate(z_partners):
                early.append(
                    send(
                        acc.at[of, p, split:rows], early_z.at[k, of], ez_send.at[n, k], ez_recv.at[n, k],
                        {"azim": p * 2 + core},
                    )
                )
    if not interleave:
        for k, g in enumerate(partners):
            scatter_to(k, g)

    for copy in back:
        copy.wait_recv()
    for copy in back_own:
        copy.wait()
    for s in range(sweeps):
        def combine(h, carry, s=s):
            at = pl.ds(pl.multiple_of(h * width, PIX), width)
            val = cot[s, at, :].astype(jnp.float32) + ret[s, at, :].astype(jnp.float32)
            store_shifted(gy, s, h, val)
            edge_left[pl.ds(s * height + h, 1), :] = val[0:1]
            edge_right[pl.ds(s * height + h, 1), :] = val[width - 1 : width]
            return carry
        lax.fori_loop(0, height, combine, 0)
    to_right = send(edge_right, in_left, halo_send.at[2], halo_recv.at[2], {"azim": right})
    to_left = send(edge_left, in_right, halo_send.at[3], halo_recv.at[3], {"azim": left})

    def fold(v):
        return sum(v[8 * i : 8 * i + 8] for i in range(1, width // 8)) + v[0:8]

    for s in range(sweeps):
        def weigh(h, carry, s=s):
            mid = gy[1, s, h + 1]
            for t in range(9):
                taps[t] = taps[t] + fold(mid * act[t % 3, s, h + t // 3])
            taps[9] = taps[9] + fold(mid)
            return carry
        lax.fori_loop(0, height, weigh, 0)
    small[...] = jnp.zeros(small.shape, jnp.float32)
    for t in range(10):
        small[t : t + 1, :] = jnp.sum(taps[t], axis=0, keepdims=True) * predivide
    small[10:11, :] = gain_total * predivide
    sp = send(small, small_pair, sp_send, sp_recv, {"azim": other})

    to_right.wait_recv()
    to_left.wait_recv()
    patch_edges(gy, in_left, in_right, sweeps, height, width)
    for s in range(sweeps):
        def convolve(h, carry, s=s):
            mid = gy[1, s, h + 1]
            total = jnp.zeros(mid.shape, jnp.float32)
            for a in range(3):
                for b in range(3):
                    t = 3 * a + b
                    total = total + kern[t : t + 1, :] * gy[2 - b, s, h + 2 - a]
            x = lat[s, h].astype(jnp.float32)
            sig = 1.0 / (1.0 + jnp.exp(-x))
            lat_out[s, h] = mid + total * (sig * (1.0 + x * (1.0 - sig)))
            return carry
        lax.fori_loop(0, height, convolve, 0)
    lat_copy = pltpu.make_async_copy(lat_out, out_lat, lat_sem)
    lat_copy.start()

    sp.wait_recv()
    small_sweep[me] = small[...] + small_pair[...]
    ss = []
    for k, g in enumerate(partners):
        ss.append(
            send(small_sweep.at[me], small_sweep.at[me], ss_send.at[k], ss_recv.at[k], {"sweep": g})
        )

    late = []
    if split < rows:
        for copy in early:
            copy.wait_recv()
        for k, g in enumerate(partners + [me]):
            for i in range(per):
                u = g * per + i
                total = acc[u, z, split:rows]
                for j in range(planes - 1):
                    total = total + early_z[j, u]
                early_sum[u] = total
            if k < groups - 1:
                late.append(
                    send(
                        early_sum.at[pl.ds(g * per, per)], late_buf.at[k], late_send.at[k], late_recv.at[k],
                        {"sweep": g},
                    )
                )
    for copy in scatter:
        copy.wait_recv()
    along = []
    for k, p in enumerate(z_partners + [z]):
        for i in range(per):
            total = acc[me * per + i, p, 0:split]
            for j in range(groups - 1):
                total = total + sweep_buf[j, i, p]
            acc2[p, i] = total
        if k < planes - 1:
            along.append(
                send(acc2.at[p], z_buf.at[k], z_send.at[k], z_recv.at[k], {"azim": p * 2 + core})
            )

    for copy in ss:
        copy.wait_recv()
    total = small_sweep[0]
    for g in range(1, groups):
        total = total + small_sweep[g]
    small_z[z] = total
    sz = []
    for k, p in enumerate(z_partners):
        sz.append(
            send(small_z.at[z], small_z.at[z], sz_send.at[k], sz_recv.at[k], {"azim": p * 2 + core})
        )

    gather = []
    if split < rows:
        for copy in late:
            copy.wait_recv()
        for i in range(per):
            total = early_sum[me * per + i]
            for k in range(groups - 1):
                total = total + late_buf[k, i]
            out_fin[me, i, split:rows] = total * predivide
        for k, g in enumerate(partners):
            some = out_fin.at[me, :, split:rows]
            gather.append(send(some, some, fin_send.at[1, k], fin_recv.at[1, k], {"sweep": g}))
    for copy in along:
        copy.wait_recv()
    for i in range(per):
        total = acc2[z, i]
        for k in range(planes - 1):
            total = total + z_buf[k, i]
        out_fin[me, i, 0:split] = total * predivide
    for k, g in enumerate(partners):
        some = out_fin.at[me, :, 0:split]
        gather.append(send(some, some, fin_send.at[0, k], fin_recv.at[0, k], {"sweep": g}))
    for copy in sz:
        copy.wait_recv()
    total = small_z[0]
    for p in range(1, planes):
        total = total + small_z[p]
    out_small[...] = total
    for copy in gather:
        copy.wait_recv()
    for copy in pending:
        copy.wait_send()
    lat_copy.wait()


def finish_kernel(parts, lat, fin, small, out_lat, out_kern, out_bias, out_gain, out_q, out_k, out_v, out_o):
    out_lat[...] = lat[...]

    @pl.when(pl.program_id(0) == 0)
    def unpack():
        groups, per, rows, _ = fin.shape
        lanes = groups * per // parts // 4
        for g in range(groups):
            for i in range(per):
                c, p = divmod(g * per + i, parts)
                out = (out_q, out_k, out_v, out_o)[c // lanes]
                j = c % lanes
                out[p * rows : (p + 1) * rows, j * LANES : (j + 1) * LANES] = fin[g, i]
        out_kern[...] = small[0:9, :]
        out_bias[...] = small[9:10, :]
        out_gain[...] = small[10:11, :]


def whole_block(shape):
    return pl.BlockSpec(shape, lambda i: (0,) * len(shape))


def on_device(
    latents, cotangent, conv_kernel, conv_bias, norm_gain, w_query, w_key, w_value, w_output
):
    f32, bf16 = jnp.float32, jnp.bfloat16
    dma = pltpu.SemaphoreType.DMA
    sds = jax.ShapeDtypeStruct
    sweeps, height, width, channels = latents.shape
    inner = w_query.shape[1]
    groups = lax.axis_size("sweep")
    strips = lax.axis_size("azim")
    planes = strips // 2
    each = height * width // groups
    total = sweeps * groups
    tokens = total * each
    edge = pltpu.VMEM((sweeps * height, channels), f32)
    framed = pltpu.VMEM((3, sweeps, height + 2, width, channels), f32)
    flat = (sweeps, height * width, channels)
    pixels = pltpu.VMEM((total, each, channels), bf16)
    lanes = inner // LANES
    chunks = 4 * lanes
    rows_each = channels // strips
    parts = max(1, groups // chunks)
    rows = rows_each // parts
    per = chunks * parts // groups
    predivide = 1.0 / math.sqrt(total * height * width * strips)
    small_shape = (16, channels)
    lines = height // groups if groups <= height else 1
    second = rows * 3 // 8 // 8 * 8
    to_sweep, to_z, one = dma((groups - 1,)), dma((planes - 1,)), dma(())

    raw_lat, fin, small = pl.pallas_call(
        functools.partial(block_kernel, groups, strips, inner // DH, predivide),
        out_shape=[
            sds(latents.shape, f32), sds((groups, per, rows, LANES), f32), sds(small_shape, f32),
        ],
        in_specs=[VMEM] * 5 + [ANY] * 4,
        out_specs=[ANY, VMEM, VMEM],
        scratch_shapes=[
            framed, framed, pltpu.VMEM(flat, bf16), pixels, pixels, pixels, pltpu.VMEM(flat, bf16),
            edge, edge, edge, edge, edge, edge, edge, edge,
            pltpu.VMEM((4, channels, inner), bf16),
            pltpu.VMEM((2, tokens, channels), bf16),
            pltpu.VMEM((4, tokens, inner), bf16),
            pltpu.VMEM((tokens, inner), bf16),
            pltpu.VMEM((4, lanes, planes, 2, parts, rows, LANES), f32),
            pltpu.VMEM((4, lanes, planes, parts, rows, LANES), f32),
            pltpu.VMEM((chunks * parts, planes, rows, LANES), f32),
            pltpu.VMEM((groups - 1, per, planes, rows - second, LANES), f32),
            pltpu.VMEM((planes, per, rows - second, LANES), f32),
            pltpu.VMEM((planes - 1, per, rows - second, LANES), f32),
            pltpu.VMEM((planes - 1, chunks * parts, max(8, second), LANES), f32),
            pltpu.VMEM((chunks * parts, max(8, second), LANES), f32),
            pltpu.VMEM((groups - 1, per, max(8, second), LANES), f32),
            pltpu.VMEM(latents.shape, f32),
            pltpu.VMEM((10, 8, channels), f32),
            pltpu.VMEM(small_shape, f32),
            pltpu.VMEM(small_shape, f32),
            pltpu.VMEM((groups,) + small_shape, f32),
            pltpu.VMEM((planes,) + small_shape, f32),
            dma((4,)), dma((2 + lines,)), dma((1 + lines, groups - 1)), dma((1 + lines, groups - 1)),
            dma((lines, groups - 1)), dma((lines, groups - 1)), dma((4,)), dma((4,)),
            dma((4,)), dma((4,)), to_sweep, to_sweep, to_z, to_z, dma((2, groups - 1)), dma((2, groups - 1)),
            one, one, to_sweep, to_sweep, to_z, to_z, one,
            dma((4, planes - 1)), dma((4, planes - 1)), to_sweep, to_sweep,
        ],
        compiler_params=pltpu.CompilerParams(
            collective_id=0, has_side_effects=True, vmem_limit_bytes=BIG
        ),
        name="block",
    )(
        latents, cotangent.reshape(flat), conv_kernel, conv_bias.reshape(1, channels),
        norm_gain.reshape(1, channels), w_query, w_key, w_value, w_output,
    )
    half = pl.BlockSpec(
        (1, height // 2, width, channels), lambda i: (lax.div(i, 2), lax.rem(i, 2), 0, 0)
    )
    out_mat, line = sds((rows_each, inner), f32), sds((1, channels), f32)
    out = pl.pallas_call(
        functools.partial(finish_kernel, parts),
        out_shape=[
            sds(latents.shape, f32), sds(conv_kernel.shape, f32), line, line,
            out_mat, out_mat, out_mat, out_mat,
        ],
        grid=(sweeps * 2,),
        in_specs=[half, whole_block(fin.shape), whole_block(small_shape)],
        out_specs=[half] + [
            whole_block(shape)
            for shape in (conv_kernel.shape, line.shape, line.shape) + (out_mat.shape,) * 4
        ],
        compiler_params=pltpu.CompilerParams(vmem_limit_bytes=BIG),
        name="finish",
    )(raw_lat, fin, small)
    grad_latents, grad_kernel, grad_bias, grad_gain, *mats = out
    return (grad_latents, grad_kernel, grad_bias.reshape(channels), grad_gain.reshape(channels), *mats)


def solution(mesh):
    image = P("sweep", None, "azim", None)
    share = P("azim", None)
    return jax.shard_map(
        on_device,
        mesh=mesh,
        in_specs=(image, image) + (P(),) * 7,
        out_specs=(image, P(), P(), P(), share, share, share, share),
        check_vma=False,
    )
```

profile of v0, /device:TPU:0, one launch (start us, length us, event | category | flops | bytes accessed | tf_op | source)
XLA Modules:
  0.0 51.3 jit_solution(5827829969805460325)
XLA Ops:
  0.6 47.0 %block.1 = (f32[2,8,32,512]{3,2,1,0:T(8,128)}, f32[4,2,64,128]{3,2,1,0:T(8,128)}, f32[16,512]{1,0:T(8,128)}) custom-call(bf16[2,8,32,512]{3,2,1,0:T(8,128)(2,1)} %lat.1, bf16[2,256,512]{2,1,0:T(8,128)(2,1)} %bitcast.5, f32[9,512]{1,0:T(8,128)} %kern.1, f32[1,512]{1,0:T(1,128)} %bitcast.6, f32[1,512]{1,0:T(1,128)} %bitcast.7, bf16[512,256]{1,0:T(8,128)(2,1)} %wq_hbm.1, ...), custom_call_target="tpu_custom_call" | custom-call | tf_op jit(solution)/shard_map/block/pallas_call | solution.py:513
  47.7 3.6 %finish.1 = (f32[2,8,32,512]{3,2,1,0:T(8,128)}, f32[9,512]{1,0:T(8,128)}, f32[1,512]{1,0:T(1,128)}, f32[1,512]{1,0:T(1,128)}, f32[64,256]{1,0:T(8,128)}, /*index...) custom-call(f32[2,8,32,512]{3,2,1,0:T(8,128)} %get-tuple-element.19.lat, ...), custom_call_target="tpu_custom_call" | custom-call | tf_op jit(solution)/shard_map/finish/pallas_call | solution.py:560
where the time goes:
time: 51.5 us; the launch traced here: 51.3 us
  Pallas kernels  50.6 us (98%)
  between operations  0.64 us (1%)
    pallas_call x1, Pallas kernels, on_device(): pl.pallas_call(functools.partial(block_kernel, groups, strips, inner // D...  47 us
    pallas_call x1, Pallas kernels, on_device(): pl.pallas_call(functools.partial(finish_kernel, parts), out_shape=[sds(la...  3.6 us

commit v1 on v0

--- a/solution.py
+++ b/solution.py
@@ -63,16 +63,17 @@
 
 
 def block_kernel(
-    groups, strips, heads, predivide,
+    groups, strips, heads, predivide, direct,
     lat, cot, kern, bias, gain_ref, wq_hbm, wk_hbm, wv_hbm, wo_hbm,
     out_lat, out_fin, out_small,
     act, gy, y_src, y_pix, cot_pix, grad, ret,
     fore_left, fore_right, fore_in_left, fore_in_right, edge_left, edge_right, in_left, in_right,
-    weights, left_s, right_s, grad_att_s, mats, pair_buf, acc, sweep_buf, acc2, z_buf, early_z, early_sum, late_buf, lat_out,
+    weights, left_s, right_s, grad_att_s, mats, pair_buf, acc, sweep_buf, sweep_sum, z_buf,
+    early_z, early_sum, late_buf, lat_out,
     taps, small, small_pair, small_sweep, small_z,
     w_sem, own_sem, a2a_send, a2a_recv, back_send, back_recv, halo_send, halo_recv,
-    pair_send, pair_recv, sweep_send, sweep_recv, z_send, z_recv, fin_send, fin_recv,
-    sp_send, sp_recv, ss_send, ss_recv, sz_send, sz_recv, lat_sem, ez_send, ez_recv, late_send, late_recv,
+    pair_send, pair_recv, one_send, one_recv, two_send, two_recv, fin_send, fin_recv,
+    sp_send, sp_recv, ss_send, ss_recv, sz_send, sz_recv, lat_sem,
 ):
     sweeps, height, width, channels = lat.shape
     each = height * width // groups
@@ -204,6 +205,91 @@
         for h in range(1, heads):
             total = jnp.where(lane_head == h, value[h * m : (h + 1) * m], total)
         return total
+
+    pairs, firsts, seconds, gather = {}, {}, {}, []
+
+    def form(i):
+        full = dot(left_s[i // 3], right_s[i], TN)
+        if not direct:
+            out_fin[i] = full
+            return
+        _, lanes, _, _, rows, _ = mats.shape
+        for j in range(lanes):
+            part = full[:, j * LANES : (j + 1) * LANES]
+            mats[i, j] = part.reshape(planes, 2, rows, LANES)
+        pairs[i] = send(
+            mats.at[i, :, :, 1 - core], pair_buf.at[i], pair_send.at[i], pair_recv.at[i], {"azim": other}
+        )
+
+    def scatter_first(i):
+        if not direct:
+            return
+        pairs[i].wait_recv()
+        _, _, _, lanes, rows, _ = acc.shape
+        for q in range(planes):
+            for g in range(groups):
+                at = slice(g * rows, (g + 1) * rows)
+                for j in range(lanes):
+                    acc[i, q, g, j] = mats[i, j, q, core, at, :] + pair_buf[i, j, q, at, :]
+        firsts[i] = []
+        if i == 3:
+            for k, p in enumerate(z_partners):
+                firsts[i].append(
+                    send(acc.at[i, p], early_z.at[k], one_send.at[i, k], one_recv.at[i, k], {"azim": p * 2 + core})
+                )
+        else:
+            for k, g in enumerate(partners):
+                firsts[i].append(
+                    send(acc.at[i, :, g], sweep_buf.at[i, k], one_send.at[i, k], one_recv.at[i, k], {"sweep": g})
+                )
+
+    def scatter_second(i):
+        if not direct:
+            return
+        for copy in firsts[i]:
+            copy.wait_recv()
+        seconds[i] = []
+        if i == 3:
+            for k, g in enumerate(partners + [me]):
+                total = acc[i, z, g]
+                for j in range(planes - 1):
+                    total = total + early_z[j, g]
+                early_sum[g] = total
+                if k < groups - 1:
+                    seconds[i].append(
+                        send(early_sum.at[g], late_buf.at[k], two_send.at[i, k], two_recv.at[i, k], {"sweep": g})
+                    )
+        else:
+            for k, p in enumerate(z_partners + [z]):
+                total = acc[i, p, me]
+                for j in range(groups - 1):
+                    total = total + sweep_buf[i, j, p]
+                sweep_sum[i, p] = total
+                if k < planes - 1:
+                    seconds[i].append(
+                        send(
+                            sweep_sum.at[i, p], z_buf.at[i, k], two_send.at[i, k], two_recv.at[i, k],
+                            {"azim": p * 2 + core},
+                        )
+                    )
+
+    def gather_final(i):
+        if not direct:
+            return
+        for copy in seconds[i]:
+            copy.wait_recv()
+        if i == 3:
+            total = early_sum[me]
+            for k in range(groups - 1):
+                total = total + late_buf[k]
+        else:
+            total = sweep_sum[i, z]
+            for k in range(planes - 1):
+                total = total + z_buf[i, k]
+        out_fin[me, i] = total * predivide
+        for k, g in enumerate(partners):
+            some = out_fin.at[me, i]
+            gather.append(send(some, some, fin_send.at[i, k], fin_recv.at[i, k], {"sweep": g}))
 
     y_own.wait()
     back, back_own = [], []
@@ -228,7 +314,7 @@
         queries = dot(normed, weights[0], NN).astype(jnp.bfloat16)
         keys = dot(normed, weights[1], NN).astype(jnp.bfloat16)
         values = dot(normed, weights[2], NN).astype(jnp.bfloat16)
-        grads = []
+        forward = []
         for i in range(several):
             part = slice(i * m, (i + 1) * m)
             own = slice((stage * several + i) * m, (stage * several + i + 1) * m)
@@ -241,16 +327,28 @@
             probs = expon / jnp.sum(expon, axis=-1, keepdims=True)
             probs_low = probs.astype(jnp.bfloat16)
             right_s[3, own, :] = collect(dot(probs_low, value, NN)).astype(jnp.bfloat16)
+            grad_v = dot(probs_low, grad_att_x, TN).astype(jnp.bfloat16)
+            right_s[2, own, :] = grad_v
+            forward.append((own, key, value, query_x, grad_att_x, probs, grad_v))
+        last = stage == lines - 1
+        if last:
+            form(3)
+            form(2)
+            scatter_first(3)
+        grads = []
+        for own, key, value, query_x, grad_att_x, probs, grad_v in forward:
             grad_probs = dot(grad_att_x, value, NT)
             inner_sum = jnp.sum(probs * grad_probs, axis=-1, keepdims=True)
             grad_scores = (probs * (grad_probs - inner_sum) * scale).astype(jnp.bfloat16)
-            grad_v = dot(probs_low, grad_att_x, TN).astype(jnp.bfloat16)
             grad_q = collect(dot(grad_scores, key, NN)).astype(jnp.bfloat16)
             grad_k = dot(grad_scores, query_x, TN).astype(jnp.bfloat16)
             right_s[0, own, :] = grad_q
             right_s[1, own, :] = grad_k
-            right_s[2, own, :] = grad_v
             grads.append((grad_q, grad_k, grad_v))
+        if last:
+            scatter_first(2)
+            form(0)
+            form(1)
         grad_q, grad_k, grad_v = (jnp.concatenate(each_grad, axis=0) for each_grad in zip(*grads))
         grad_normed = (
             dot(grad_q, weights[0], NT) + dot(grad_k, weights[1], NT) + dot(grad_v, weights[2], NT)
@@ -276,48 +374,8 @@
         )
         back_own[-1].start()
 
-    _, lanes, _, _, parts, rows, _ = mats.shape
-    per = 4 * lanes * parts // groups
-    interleave = groups == 4
-    order = [lax.rem(me + k + 1, 4) if interleave else k for k in range(4)]
-    pairs = []
-    for n, i in enumerate(order):
-        full = dot(left_s[i // 3], right_s[i], TN)
-        for j in range(lanes):
-            part = full[:, j * LANES : (j + 1) * LANES]
-            mats[i, j] = part.reshape(planes, 2, parts, rows, LANES)
-        pairs.append(
-            send(mats.at[i, :, :, 1 - core], pair_buf.at[i], pair_send.at[n], pair_recv.at[n], {"azim": other})
-        )
-    scatter, early = [], []
-    units = lanes * parts
-    split = rows - rows * 3 // 8 // 8 * 8
-
-    def scatter_to(k, g):
-        scatter.append(
-            send(acc.at[pl.ds(g * per, per), :, 0:split], sweep_buf.at[k], sweep_send.at[k], sweep_recv.at[k], {"sweep": g})
-        )
-
-    for n, i in enumerate(order):
-        pairs[n].wait_recv()
-        for j in range(lanes):
-            for p in range(parts):
-                for q in range(planes):
-                    acc[(i * lanes + j) * parts + p, q] = mats[i, j, q, core, p] + pair_buf[i, j, q, p]
-        if interleave and n < 3:
-            scatter_to(n, i)
-        if split < rows:
-            of = pl.ds(i * units, units)
-            for k, p in enumerate(z_partners):
-                early.append(
-                    send(
-                        acc.at[of, p, split:rows], early_z.at[k, of], ez_send.at[n, k], ez_recv.at[n, k],
-                        {"azim": p * 2 + core},
-                    )
-                )
-    if not interleave:
-        for k, g in enumerate(partners):
-            scatter_to(k, g)
+    scatter_first(0)
+    scatter_first(1)
 
     for copy in back:
         copy.wait_recv()
@@ -335,6 +393,8 @@
     to_right = send(edge_right, in_left, halo_send.at[2], halo_recv.at[2], {"azim": right})
     to_left = send(edge_left, in_right, halo_send.at[3], halo_recv.at[3], {"azim": left})
 
+    scatter_second(2)
+
     def fold(v):
         return sum(v[8 * i : 8 * i + 8] for i in range(1, width // 8)) + v[0:8]
 
@@ -352,6 +412,7 @@
     small[10:11, :] = gain_total * predivide
     sp = send(small, small_pair, sp_send, sp_recv, {"azim": other})
 
+    scatter_second(3)
     to_right.wait_recv()
     to_left.wait_recv()
     patch_edges(gy, in_left, in_right, sweeps, height, width)
@@ -371,6 +432,8 @@
     lat_copy = pltpu.make_async_copy(lat_out, out_lat, lat_sem)
     lat_copy.start()
 
+    scatter_second(0)
+    gather_final(3)
     sp.wait_recv()
     small_sweep[me] = small[...] + small_pair[...]
     ss = []
@@ -379,38 +442,8 @@
             send(small_sweep.at[me], small_sweep.at[me], ss_send.at[k], ss_recv.at[k], {"sweep": g})
         )
 
-    late = []
-    if split < rows:
-        for copy in early:
-            copy.wait_recv()
-        for k, g in enumerate(partners + [me]):
-            for i in range(per):
-                u = g * per + i
-                total = acc[u, z, split:rows]
-                for j in range(planes - 1):
-                    total = total + early_z[j, u]
-                early_sum[u] = total
-            if k < groups - 1:
-                late.append(
-                    send(
-                        early_sum.at[pl.ds(g * per, per)], late_buf.at[k], late_send.at[k], late_recv.at[k],
-                        {"sweep": g},
-                    )
-                )
-    for copy in scatter:
-        copy.wait_recv()
-    along = []
-    for k, p in enumerate(z_partners + [z]):
-        for i in range(per):
-            total = acc[me * per + i, p, 0:split]
-            for j in range(groups - 1):
-                total = total + sweep_buf[j, i, p]
-            acc2[p, i] = total
-        if k < planes - 1:
-            along.append(
-                send(acc2.at[p], z_buf.at[k], z_send.at[k], z_recv.at[k], {"azim": p * 2 + core})
-            )
-
+    scatter_second(1)
+    gather_final(2)
     for copy in ss:
         copy.wait_recv()
     total = small_sweep[0]
@@ -423,28 +456,8 @@
             send(small_z.at[z], small_z.at[z], sz_send.at[k], sz_recv.at[k], {"azim": p * 2 + core})
         )
 
-    gather = []
-    if split < rows:
-        for copy in late:
-            copy.wait_recv()
-        for i in range(per):
-            total = early_sum[me * per + i]
-            for k in range(groups - 1):
-                total = total + late_buf[k, i]
-            out_fin[me, i, split:rows] = total * predivide
-        for k, g in enumerate(partners):
-            some = out_fin.at[me, :, split:rows]
-            gather.append(send(some, some, fin_send.at[1, k], fin_recv.at[1, k], {"sweep": g}))
-    for copy in along:
-        copy.wait_recv()
-    for i in range(per):
-        total = acc2[z, i]
-        for k in range(planes - 1):
-            total = total + z_buf[k, i]
-        out_fin[me, i, 0:split] = total * predivide
-    for k, g in enumerate(partners):
-        some = out_fin.at[me, :, 0:split]
-        gather.append(send(some, some, fin_send.at[0, k], fin_recv.at[0, k], {"sweep": g}))
+    gather_final(0)
+    gather_final(1)
     for copy in sz:
         copy.wait_recv()
     total = small_z[0]
@@ -458,19 +471,19 @@
     lat_copy.wait()
 
 
-def finish_kernel(parts, lat, fin, small, out_lat, out_kern, out_bias, out_gain, out_q, out_k, out_v, out_o):
+def finish_kernel(lat, fin, small, out_lat, out_kern, out_bias, out_gain, out_q, out_k, out_v, out_o):
     out_lat[...] = lat[...]
 
     @pl.when(pl.program_id(0) == 0)
     def unpack():
-        groups, per, rows, _ = fin.shape
-        lanes = groups * per // parts // 4
-        for g in range(groups):
-            for i in range(per):
-                c, p = divmod(g * per + i, parts)
-                out = (out_q, out_k, out_v, out_o)[c // lanes]
-                j = c % lanes
-                out[p * rows : (p + 1) * rows, j * LANES : (j + 1) * LANES] = fin[g, i]
+        for i, out in enumerate((out_q, out_k, out_v, out_o)):
+            if len(fin.shape) == 3:
+                out[...] = fin[i]
+            else:
+                groups, _, lanes, rows, _ = fin.shape
+                for g in range(groups):
+                    for j in range(lanes):
+                        out[g * rows : (g + 1) * rows, j * LANES : (j + 1) * LANES] = fin[g, i, j]
         out_kern[...] = small[0:9, :]
         out_bias[...] = small[9:10, :]
         out_gain[...] = small[10:11, :]
@@ -499,21 +512,21 @@
     flat = (sweeps, height * width, channels)
     pixels = pltpu.VMEM((total, each, channels), bf16)
     lanes = inner // LANES
-    chunks = 4 * lanes
     rows_each = channels // strips
-    parts = max(1, groups // chunks)
-    rows = rows_each // parts
-    per = chunks * parts // groups
+    direct = rows_each % (8 * groups) == 0
+    rows = rows_each // groups if direct else 8
+    fin_shape = (groups, 4, lanes, rows, LANES) if direct else (4, channels, inner)
+    share = (lanes, rows, LANES)
+    most = max(groups, planes) - 1
     predivide = 1.0 / math.sqrt(total * height * width * strips)
     small_shape = (16, channels)
     lines = height // groups if groups <= height else 1
-    second = rows * 3 // 8 // 8 * 8
     to_sweep, to_z, one = dma((groups - 1,)), dma((planes - 1,)), dma(())
 
     raw_lat, fin, small = pl.pallas_call(
-        functools.partial(block_kernel, groups, strips, inner // DH, predivide),
+        functools.partial(block_kernel, groups, strips, inner // DH, predivide, direct),
         out_shape=[
-            sds(latents.shape, f32), sds((groups, per, rows, LANES), f32), sds(small_shape, f32),
+            sds(latents.shape, f32), sds(fin_shape, f32), sds(small_shape, f32),
         ],
         in_specs=[VMEM] * 5 + [ANY] * 4,
         out_specs=[ANY, VMEM, VMEM],
@@ -524,15 +537,15 @@
             pltpu.VMEM((2, tokens, channels), bf16),
             pltpu.VMEM((4, tokens, inner), bf16),
             pltpu.VMEM((tokens, inner), bf16),
-            pltpu.VMEM((4, lanes, planes, 2, parts, rows, LANES), f32),
-            pltpu.VMEM((4, lanes, planes, parts, rows, LANES), f32),
-            pltpu.VMEM((chunks * parts, planes, rows, LANES), f32),
-            pltpu.VMEM((groups - 1, per, planes, rows - second, LANES), f32),
-            pltpu.VMEM((planes, per, rows - second, LANES), f32),
-            pltpu.VMEM((planes - 1, per, rows - second, LANES), f32),
-            pltpu.VMEM((planes - 1, chunks * parts, max(8, second), LANES), f32),
-            pltpu.VMEM((chunks * parts, max(8, second), LANES), f32),
-            pltpu.VMEM((groups - 1, per, max(8, second), LANES), f32),
+            pltpu.VMEM((4, lanes, planes, 2, groups * rows, LANES), f32),
+            pltpu.VMEM((4, lanes, planes, groups * rows, LANES), f32),
+            pltpu.VMEM((4, planes, groups) + share, f32),
+            pltpu.VMEM((3, groups - 1, planes) + share, f32),
+            pltpu.VMEM((3, planes) + share, f32),
+            pltpu.VMEM((3, planes - 1) + share, f32),
+            pltpu.VMEM((planes - 1, groups) + share, f32),
+            pltpu.VMEM((groups,) + share, f32),
+            pltpu.VMEM((groups - 1,) + share, f32),
             pltpu.VMEM(latents.shape, f32),
             pltpu.VMEM((10, 8, channels), f32),
             pltpu.VMEM(small_shape, f32),
@@ -541,9 +554,9 @@
             pltpu.VMEM((planes,) + small_shape, f32),
             dma((4,)), dma((2 + lines,)), dma((1 + lines, groups - 1)), dma((1 + lines, groups - 1)),
             dma((lines, groups - 1)), dma((lines, groups - 1)), dma((4,)), dma((4,)),
-            dma((4,)), dma((4,)), to_sweep, to_sweep, to_z, to_z, dma((2, groups - 1)), dma((2, groups - 1)),
+            dma((4,)), dma((4,)), dma((4, most)), dma((4, most)), dma((4, most)), dma((4, most)),
+            dma((4, groups - 1)), dma((4, groups - 1)),
             one, one, to_sweep, to_sweep, to_z, to_z, one,
-            dma((4, planes - 1)), dma((4, planes - 1)), to_sweep, to_sweep,
         ],
         compiler_params=pltpu.CompilerParams(
             collective_id=0, has_side_effects=True, vmem_limit_bytes=BIG
@@ -553,12 +566,15 @@
         latents, cotangent.reshape(flat), conv_kernel, conv_bias.reshape(1, channels),
         norm_gain.reshape(1, channels), w_query, w_key, w_value, w_output,
     )
+    if not direct:
+        fin = lax.psum_scatter(fin * predivide, "azim", scatter_dimension=1, tiled=True)
+        fin = lax.psum(fin, "sweep")
     half = pl.BlockSpec(
         (1, height // 2, width, channels), lambda i: (lax.div(i, 2), lax.rem(i, 2), 0, 0)
     )
     out_mat, line = sds((rows_each, inner), f32), sds((1, channels), f32)
     out = pl.pallas_call(
-        functools.partial(finish_kernel, parts),
+        finish_kernel,
         out_shape=[
             sds(latents.shape, f32), sds(conv_kernel.shape, f32), line, line,
             out_mat, out_mat, out_mat, out_mat,

time: 51.5 us -> 53.6 us (1.041)
  Pallas kernels: 50.6 us -> 52.7 us
    pallas_call x1, Pallas kernels: 47 us -> 49.1 us  [on_device(): pl.pallas_call(functools.partial(block_kernel, groups, strips, inner // D...]
where the time goes in v1:
time: 53.6 us; the launch traced here: 53.3 us
  Pallas kernels  52.7 us (98%)
  between operations  0.64 us (1%)
    pallas_call x1, Pallas kernels, on_device(): pl.pallas_call(functools.partial(block_kernel, groups, strips, inner // D...  49.1 us
    pallas_call x1, Pallas kernels, on_device(): pl.pallas_call(finish_kernel, out_shape=[sds(latents.shape, f32), sds(con...  3.6 us

profile of v1, /device:TPU:0, one launch (start us, length us, event | category | flops | bytes accessed | tf_op | source)
XLA Modules:
  0.0 53.3 jit_solution(10285360965761360017)
XLA Ops:
  0.6 49.1 %block.1 = (f32[2,8,32,512]{3,2,1,0:T(8,128)}, f32[4,4,2,16,128]{4,3,2,1,0:T(8,128)}, f32[16,512]{1,0:T(8,128)}) custom-call(bf16[2,8,32,512]{3,2,1,0:T(8,128)(2,1)} %lat.1, bf16[2,256,512]{2,1,0:T(8,128)(2,1)} %bitcast.5, f32[9,512]{1,0:T(8,128)} %kern.1, f32[1,512]{1,0:T(1,128)} %bitcast.6, f32[1,512]{1,0:T(1,128)} %bitcast.7, bf16[512,256]{1,0:T(8,128)(2,1)} %wq_hbm.1, ...), custom_call_target="tpu_custom_call" | custom-call | tf_op jit(solution)/shard_map/block/pallas_call | solution.py:526
  49.7 3.6 %finish.1 = (f32[2,8,32,512]{3,2,1,0:T(8,128)}, f32[9,512]{1,0:T(8,128)}, f32[1,512]{1,0:T(1,128)}, f32[1,512]{1,0:T(1,128)}, f32[64,256]{1,0:T(8,128)}, /*index...) custom-call(f32[2,8,32,512]{3,2,1,0:T(8,128)} %get-tuple-element.19.lat, ...), custom_call_target="tpu_custom_call" | custom-call | tf_op jit(solution)/shard_map/finish/pallas_call | solution.py:576

commit v2 on v0

--- a/solution.py
+++ b/solution.py
@@ -28,7 +28,10 @@
     barrier = pltpu.get_barrier_semaphore()
     for where in partners:
         pl.semaphore_signal(barrier, inc=1, device_id=where, device_id_type=MESH)
-    pl.semaphore_wait(barrier, len(partners))
+
+
+def await_greetings(count):
+    pl.semaphore_wait(pltpu.get_barrier_semaphore(), count)
 
 
 def store_shifted(dst, s, h, val):
@@ -64,15 +67,15 @@
 
 def block_kernel(
     groups, strips, heads, predivide,
-    lat, cot, kern, bias, gain_ref, wq_hbm, wk_hbm, wv_hbm, wo_hbm,
+    lat_hbm, cot_hbm, kern_hbm, bias_hbm, gain_hbm, wq_hbm, wk_hbm, wv_hbm, wo_hbm,
     out_lat, out_fin, out_small,
-    act, gy, y_src, y_pix, cot_pix, grad, ret,
+    lat, cot, kern, bias, gain_ref, act, gy, y_src, y_pix, cot_pix, grad, ret,
     fore_left, fore_right, fore_in_left, fore_in_right, edge_left, edge_right, in_left, in_right,
     weights, left_s, right_s, grad_att_s, mats, pair_buf, acc, sweep_buf, acc2, z_buf, early_z, early_sum, late_buf, lat_out,
     taps, small, small_pair, small_sweep, small_z,
     w_sem, own_sem, a2a_send, a2a_recv, back_send, back_recv, halo_send, halo_recv,
     pair_send, pair_recv, sweep_send, sweep_recv, z_send, z_recv, fin_send, fin_recv,
-    sp_send, sp_recv, ss_send, ss_recv, sz_send, sz_recv, lat_sem, ez_send, ez_recv, late_send, late_recv,
+    sp_send, sp_recv, ss_send, ss_recv, sz_send, sz_recv, lat_sem, in_sem, ez_send, ez_recv, late_send, late_recv,
 ):
     sweeps, height, width, channels = lat.shape
     each = height * width // groups
@@ -94,23 +97,32 @@
         pending.append(copy)
         return copy
 
+    greetings = (
+        [{"sweep": g} for g in partners]
+        + [{"azim": left}, {"azim": right}, {"azim": other}]
+        + [{"azim": p * 2 + core} for p in z_partners]
+    )
+    greet(greetings)
+    inputs = []
+    for i, (source, target) in enumerate(
+        ((lat_hbm, lat), (cot_hbm, cot), (kern_hbm, kern), (bias_hbm, bias), (gain_hbm, gain_ref))
+    ):
+        inputs.append(pltpu.make_async_copy(source, target, in_sem.at[i]))
+        inputs[-1].start()
     loads = []
     for i, w in enumerate((wq_hbm, wk_hbm, wv_hbm, wo_hbm)):
         loads.append(pltpu.make_async_copy(w, weights.at[i], w_sem.at[i]))
         loads[-1].start()
-    greet(
-        [{"sweep": g} for g in partners]
-        + [{"azim": left}, {"azim": right}, {"azim": other}]
-        + [{"azim": p * 2 + core} for p in z_partners]
-    )
     mine = pl.ds(pl.multiple_of(me * each, PIX), each)
     slots = pl.ds(me * sweeps, sweeps)
 
+    inputs[0].wait()
     for s in range(sweeps):
         for h in range(height):
             i = s * height + h
             fore_left[i : i + 1, :] = lat[s, h, 0:16, :].astype(jnp.float32)[0:1]
             fore_right[i : i + 1, :] = lat[s, h, width - 16 : width, :].astype(jnp.float32)[15:16]
+    await_greetings(len(greetings))
     to_right = send(fore_right, fore_in_left, halo_send.at[0], halo_recv.at[0], {"azim": right})
     to_left = send(fore_left, fore_in_right, halo_send.at[1], halo_recv.at[1], {"azim": left})
 
@@ -119,10 +131,13 @@
         here = slice(stage * count, (stage + 1) * count)
         return send(source.at[:, there, :], target.at[slots, here, :], send_sem, recv_sem, {"sweep": g})
 
+    inputs[1].wait()
     cot_copies = [give(k, g, cot, cot_pix, 0, each, a2a_send.at[0, k], a2a_recv.at[0, k]) for k, g in enumerate(partners)]
     cot_own = pltpu.make_async_copy(cot.at[:, mine, :], cot_pix.at[slots], own_sem.at[0])
     cot_own.start()
 
+    for copy in inputs[2:]:
+        copy.wait()
     for s in range(sweeps):
         def activate(h, carry, s=s):
             x = lat[s, h].astype(jnp.float32)
@@ -280,8 +295,19 @@
     per = 4 * lanes * parts // groups
     interleave = groups == 4
     order = [lax.rem(me + k + 1, 4) if interleave else k for k in range(4)]
+    scatter, early = [], []
+    units = lanes * parts
+    split = rows - rows * 3 // 8 // 8 * 8
+
+    def scatter_to(k, g):
+        scatter.append(
+            send(acc.at[pl.ds(g * per, per), :, 0:split], sweep_buf.at[k], sweep_send.at[k], sweep_recv.at[k], {"sweep": g})
+        )
+
     pairs = []
-    for n, i in enumerate(order):
+
+    def form(n):
+        i = order[n]
         full = dot(left_s[i // 3], right_s[i], TN)
         for j in range(lanes):
             part = full[:, j * LANES : (j + 1) * LANES]
@@ -289,16 +315,12 @@
         pairs.append(
             send(mats.at[i, :, :, 1 - core], pair_buf.at[i], pair_send.at[n], pair_recv.at[n], {"azim": other})
         )
-    scatter, early = [], []
-    units = lanes * parts
-    split = rows - rows * 3 // 8 // 8 * 8
-
-    def scatter_to(k, g):
-        scatter.append(
-            send(acc.at[pl.ds(g * per, per), :, 0:split], sweep_buf.at[k], sweep_send.at[k], sweep_recv.at[k], {"sweep": g})
-        )
-
+
+    form(0)
+    form(1)
     for n, i in enumerate(order):
+        if n + 2 < 4:
+            form(n + 2)
         pairs[n].wait_recv()
         for j in range(lanes):
             for p in range(parts):
@@ -351,33 +373,6 @@
         small[t : t + 1, :] = jnp.sum(taps[t], axis=0, keepdims=True) * predivide
     small[10:11, :] = gain_total * predivide
     sp = send(small, small_pair, sp_send, sp_recv, {"azim": other})
-
-    to_right.wait_recv()
-    to_left.wait_recv()
-    patch_edges(gy, in_left, in_right, sweeps, height, width)
-    for s in range(sweeps):
-        def convolve(h, carry, s=s):
-            mid = gy[1, s, h + 1]
-            total = jnp.zeros(mid.shape, jnp.float32)
-            for a in range(3):
-                for b in range(3):
-                    t = 3 * a + b
-                    total = total + kern[t : t + 1, :] * gy[2 - b, s, h + 2 - a]
-            x = lat[s, h].astype(jnp.float32)
-            sig = 1.0 / (1.0 + jnp.exp(-x))
-            lat_out[s, h] = mid + total * (sig * (1.0 + x * (1.0 - sig)))
-            return carry
-        lax.fori_loop(0, height, convolve, 0)
-    lat_copy = pltpu.make_async_copy(lat_out, out_lat, lat_sem)
-    lat_copy.start()
-
-    sp.wait_recv()
-    small_sweep[me] = small[...] + small_pair[...]
-    ss = []
-    for k, g in enumerate(partners):
-        ss.append(
-            send(small_sweep.at[me], small_sweep.at[me], ss_send.at[k], ss_recv.at[k], {"sweep": g})
-        )
 
     late = []
     if split < rows:
@@ -410,6 +405,33 @@
             along.append(
                 send(acc2.at[p], z_buf.at[k], z_send.at[k], z_recv.at[k], {"azim": p * 2 + core})
             )
+
+    sp.wait_recv()
+    small_sweep[me] = small[...] + small_pair[...]
+    ss = []
+    for k, g in enumerate(partners):
+        ss.append(
+            send(small_sweep.at[me], small_sweep.at[me], ss_send.at[k], ss_recv.at[k], {"sweep": g})
+        )
+
+    to_right.wait_recv()
+    to_left.wait_recv()
+    patch_edges(gy, in_left, in_right, sweeps, height, width)
+    for s in range(sweeps):
+        def convolve(h, carry, s=s):
+            mid = gy[1, s, h + 1]
+            total = jnp.zeros(mid.shape, jnp.float32)
+            for a in range(3):
+                for b in range(3):
+                    t = 3 * a + b
+                    total = total + kern[t : t + 1, :] * gy[2 - b, s, h + 2 - a]
+            x = lat[s, h].astype(jnp.float32)
+            sig = 1.0 / (1.0 + jnp.exp(-x))
+            lat_out[s, h] = mid + total * (sig * (1.0 + x * (1.0 - sig)))
+            return carry
+        lax.fori_loop(0, height, convolve, 0)
+    lat_copy = pltpu.make_async_copy(lat_out, out_lat, lat_sem)
+    lat_copy.start()
 
     for copy in ss:
         copy.wait_recv()
@@ -515,9 +537,11 @@
         out_shape=[
             sds(latents.shape, f32), sds((groups, per, rows, LANES), f32), sds(small_shape, f32),
         ],
-        in_specs=[VMEM] * 5 + [ANY] * 4,
+        in_specs=[ANY] * 9,
         out_specs=[ANY, VMEM, VMEM],
         scratch_shapes=[
+            pltpu.VMEM(latents.shape, bf16), pltpu.VMEM(flat, bf16), pltpu.VMEM(conv_kernel.shape, f32),
+            pltpu.VMEM((1, channels), f32), pltpu.VMEM((1, channels), f32),
             framed, framed, pltpu.VMEM(flat, bf16), pixels, pixels, pixels, pltpu.VMEM(flat, bf16),
             edge, edge, edge, edge, edge, edge, edge, edge,
             pltpu.VMEM((4, channels, inner), bf16),
@@ -542,7 +566,7 @@
             dma((4,)), dma((2 + lines,)), dma((1 + lines, groups - 1)), dma((1 + lines, groups - 1)),
             dma((lines, groups - 1)), dma((lines, groups - 1)), dma((4,)), dma((4,)),
             dma((4,)), dma((4,)), to_sweep, to_sweep, to_z, to_z, dma((2, groups - 1)), dma((2, groups - 1)),
-            one, one, to_sweep, to_sweep, to_z, to_z, one,
+            one, one, to_sweep, to_sweep, to_z, to_z, one, dma((5,)),
             dma((4, planes - 1)), dma((4, planes - 1)), to_sweep, to_sweep,
         ],
         compiler_params=pltpu.CompilerParams(

time: 51.5 us -> 49 us (0.951)
  Pallas kernels: 50.6 us -> 48.1 us
    pallas_call x1, Pallas kernels: 47 us -> 44.6 us  [on_device(): pl.pallas_call(functools.partial(block_kernel, groups, strips, inner // D...]
where the time goes in v2:
time: 49 us; the launch traced here: 48.8 us
  Pallas kernels  48.1 us (98%)
  between operations  0.64 us (1%)
    pallas_call x1, Pallas kernels, on_device(): pl.pallas_call(functools.partial(block_kernel, groups, strips, inner // D...  44.6 us
    pallas_call x1, Pallas kernels, on_device(): pl.pallas_call(functools.partial(finish_kernel, parts), out_shape=[sds(la...  3.6 us

profile of v2, /device:TPU:0, one launch (start us, length us, event | category | flops | bytes accessed | tf_op | source)
XLA Modules:
  0.0 48.8 jit_solution(17618142235306505108)
XLA Ops:
  0.6 44.6 %block.1 = (f32[2,8,32,512]{3,2,1,0:T(8,128)}, f32[4,2,64,128]{3,2,1,0:T(8,128)}, f32[16,512]{1,0:T(8,128)}) custom-call(bf16[2,8,32,512]{3,2,1,0:T(8,128)(2,1)} %lat_hbm.1, bf16[2,256,512]{2,1,0:T(8,128)(2,1)} %bitcast.5, f32[9,512]{1,0:T(8,128)} %kern_hbm.1, f32[1,512]{1,0:T(1,128)} %bitcast.6, f32[1,512]{1,0:T(1,128)} %bitcast.7, ...), custom_call_target="tpu_custom_call" | custom-call | tf_op jit(solution)/shard_map/block/pallas_call | solution.py:535
  45.2 3.6 %finish.1 = (f32[2,8,32,512]{3,2,1,0:T(8,128)}, f32[9,512]{1,0:T(8,128)}, f32[1,512]{1,0:T(1,128)}, f32[1,512]{1,0:T(1,128)}, f32[64,256]{1,0:T(8,128)}, /*index...) custom-call(f32[2,8,32,512]{3,2,1,0:T(8,128)} %get-tuple-element.19.lat, ...), custom_call_target="tpu_custom_call" | custom-call | tf_op jit(solution)/shard_map/finish/pallas_call | solution.py:584

commit v3 on v2

--- a/solution.py
+++ b/solution.py
@@ -15,7 +15,9 @@
 MESH = pl.DeviceIdType.MESH
 VMEM = pl.BlockSpec(memory_space=pltpu.VMEM)
 ANY = pl.BlockSpec(memory_space=pl.ANY)
-BIG = 56 * 1024 * 1024
+HBM = pl.BlockSpec(memory_space=pltpu.HBM)
+MIB = 1024 * 1024
+BIG = 56 * MIB
 
 
 def remote(src, dst, send, recv, where):
@@ -537,7 +539,7 @@
         out_shape=[
             sds(latents.shape, f32), sds((groups, per, rows, LANES), f32), sds(small_shape, f32),
         ],
-        in_specs=[ANY] * 9,
+        in_specs=[HBM] * 9,
         out_specs=[ANY, VMEM, VMEM],
         scratch_shapes=[
             pltpu.VMEM(latents.shape, bf16), pltpu.VMEM(flat, bf16), pltpu.VMEM(conv_kernel.shape, f32),
@@ -570,7 +572,7 @@
             dma((4, planes - 1)), dma((4, planes - 1)), to_sweep, to_sweep,
         ],
         compiler_params=pltpu.CompilerParams(
-            collective_id=0, has_side_effects=True, vmem_limit_bytes=BIG
+            collective_id=0, has_side_effects=True, vmem_limit_bytes=BIG if total > 8 else 32 * MIB
         ),
         name="block",
     )(
@@ -578,7 +580,7 @@
         norm_gain.reshape(1, channels), w_query, w_key, w_value, w_output,
     )
     half = pl.BlockSpec(
-        (1, height // 2, width, channels), lambda i: (lax.div(i, 2), lax.rem(i, 2), 0, 0)
+        (1, height, width, channels), lambda i: (i, 0, 0, 0)
     )
     out_mat, line = sds((rows_each, inner), f32), sds((1, channels), f32)
     out = pl.pallas_call(
@@ -587,13 +589,13 @@
             sds(latents.shape, f32), sds(conv_kernel.shape, f32), line, line,
             out_mat, out_mat, out_mat, out_mat,
         ],
-        grid=(sweeps * 2,),
+        grid=(sweeps,),
         in_specs=[half, whole_block(fin.shape), whole_block(small_shape)],
         out_specs=[half] + [
             whole_block(shape)
             for shape in (conv_kernel.shape, line.shape, line.shape) + (out_mat.shape,) * 4
         ],
-        compiler_params=pltpu.CompilerParams(vmem_limit_bytes=BIG),
+        compiler_params=pltpu.CompilerParams(vmem_limit_bytes=16 * MIB),
         name="finish",
     )(raw_lat, fin, small)
     grad_latents, grad_kernel, grad_bias, grad_gain, *mats = out

time: 49 us -> 53.3 us (1.088)
  local copies, waits for them, and re-layouts: 0 us -> 7.32 us
  Pallas kernels: 48.1 us -> 44.9 us
    unnamed x0 -> x18, local copies, waits for them, and re-layouts: none -> 7.32 us
    pallas_call x1, Pallas kernels: 3.6 us -> 1.16 us  [on_device(): pl.pallas_call(functools.partial(finish_kernel, parts), out_shape=[sds(la...]
    pallas_call x1, Pallas kernels: 44.6 us -> 43.7 us  [on_device(): pl.pallas_call(functools.partial(block_kernel, groups, strips, inner // D...]
where the time goes in v3:
time: 53.3 us; the launch traced here: 52.9 us
  Pallas kernels  44.9 us (84%)
  local copies, waits for them, and re-layouts  7.32 us (14%)
  between operations  0.67 us (1%)
    pallas_call x1, Pallas kernels, on_device(): pl.pallas_call(functools.partial(block_kernel, groups, strips, inner // D...  43.7 us
    unnamed x18, local copies, waits for them, and re-layouts  7.32 us
    pallas_call x1, Pallas kernels, on_device(): pl.pallas_call(functools.partial(finish_kernel, parts), out_shape=[sds(la...  1.16 us

profile of v3, /device:TPU:0, one launch (start us, length us, event | category | flops | bytes accessed | tf_op | source)
XLA Modules:
  0.0 52.9 jit_solution(15266595602395649302)
XLA Ops:
  0.6 0.0 copy-start.8
  0.6 0.0 copy-start.7
  0.7 0.7 %copy-done.8 = f32[512]{0:T(512)S(1)} copy-done((f32[512]{0:T(512)S(1)}, f32[512]{0:T(512)}, u32[]{:S(2)}) %copy-start.8) | copy-done | bytes 2072
  1.3 0.0 copy-done.7
  1.3 0.0 copy-start
  1.3 1.0 %copy-done = bf16[2,8,32,512]{3,2,1,0:T(8,128)(2,1)S(1)} copy-done((bf16[2,8,32,512]{3,2,1,0:T(8,128)(2,1)S(1)}, bf16[2,8,32,512]{3,2,1,0:T(8,128)(2,1)}, u32[]{:S(2)}) %copy-start) | copy-done | bytes 524312
  2.4 0.0 copy-start.1
  2.4 1.0 %copy-done.1 = bf16[2,8,32,512]{3,2,1,0:T(8,128)(2,1)S(1)} copy-done((bf16[2,8,32,512]{3,2,1,0:T(8,128)(2,1)S(1)}, bf16[2,8,32,512]{3,2,1,0:T(8,128)(2,1)}, u32[]{:S(2)}) %copy-start.1) | copy-done | bytes 524312
  3.4 0.0 copy-start.2
  3.4 0.9 %copy-done.2 = bf16[512,256]{1,0:T(8,128)(2,1)S(1)} copy-done((bf16[512,256]{1,0:T(8,128)(2,1)S(1)}, bf16[512,256]{1,0:T(8,128)(2,1)}, u32[]{:S(2)}) %copy-start.2) | copy-done | bytes 262168
  4.4 0.0 copy-start.3
  4.4 0.9 %copy-done.3 = bf16[512,256]{1,0:T(8,128)(2,1)S(1)} copy-done((bf16[512,256]{1,0:T(8,128)(2,1)S(1)}, bf16[512,256]{1,0:T(8,128)(2,1)}, u32[]{:S(2)}) %copy-start.3) | copy-done | bytes 262168
  5.3 0.0 copy-start.4
  5.3 0.9 %copy-done.4 = bf16[512,256]{1,0:T(8,128)(2,1)S(1)} copy-done((bf16[512,256]{1,0:T(8,128)(2,1)S(1)}, bf16[512,256]{1,0:T(8,128)(2,1)}, u32[]{:S(2)}) %copy-start.4) | copy-done | bytes 262168
  6.3 0.0 copy-start.5
  6.3 0.9 %copy-done.5 = bf16[512,256]{1,0:T(8,128)(2,1)S(1)} copy-done((bf16[512,256]{1,0:T(8,128)(2,1)S(1)}, bf16[512,256]{1,0:T(8,128)(2,1)}, u32[]{:S(2)}) %copy-start.5) | copy-done | bytes 262168
  7.2 0.0 copy-start.6
  7.2 0.8 %copy-done.6 = f32[9,512]{1,0:T(8,128)S(1)} copy-done((f32[9,512]{1,0:T(8,128)S(1)}, f32[9,512]{1,0:T(8,128)}, u32[]{:S(2)}) %copy-start.6) | copy-done | bytes 18456
  8.0 43.7 %block.1 = (f32[2,8,32,512]{3,2,1,0:T(8,128)S(1)}, f32[4,2,64,128]{3,2,1,0:T(8,128)S(1)}, f32[16,512]{1,0:T(8,128)S(1)}) custom-call(bf16[2,8,32,512]{3,2,1,0:T(8,128)(2,1)S(1)} %copy-done, bf16[2,256,512]{2,1,0:T(8,128)(2,1)S(1)} %bitcast.5, f32[9,512]{1,0:T(8,128)S(1)} %copy-done.6, f32[1,512]{1,0:T(1,128)S(1)} %bitcast.6, f32[1,512]{1,0:T(1,128)S(1)} %bitcast.7, ...), custom_call_target="tpu_custom_call" | custom-call | tf_op jit(solution)/shard_map/block/pallas_call | solution.py:537
  51.7 1.2 %finish.1 = (f32[2,8,32,512]{3,2,1,0:T(8,128)}, f32[9,512]{1,0:T(8,128)}, f32[1,512]{1,0:T(1,128)}, f32[1,512]{1,0:T(1,128)}, f32[64,256]{1,0:T(8,128)}, /*index...) custom-call(f32[2,8,32,512]{3,2,1,0:T(8,128)S(1)} %get-tuple-element.19.lat, ...), custom_call_target="tpu_custom_call" | custom-call | tf_op jit(solution)/shard_map/finish/pallas_call | solution.py:586
Async XLA Ops:
  0.6 0.7 %copy-start.8 = (f32[512]{0:T(512)S(1)}, f32[512]{0:T(512)}, u32[]{:S(2)}) copy-start(f32[512]{0:T(512)} %param.13) | copy-start | bytes 6148
  0.6 0.7 %copy-start.7 = (f32[512]{0:T(512)S(1)}, f32[512]{0:T(512)}, u32[]{:S(2)}) copy-start(f32[512]{0:T(512)} %param.12) | copy-start | bytes 6148
  1.3 1.0 %copy-start = (bf16[2,8,32,512]{3,2,1,0:T(8,128)(2,1)S(1)}, bf16[2,8,32,512]{3,2,1,0:T(8,128)(2,1)}, u32[]{:S(2)}) copy-start(bf16[2,8,32,512]{3,2,1,0:T(8,128)(2,1)} %lat_hbm.1) | copy-start | bytes 1572868
  2.4 1.0 %copy-start.1 = (bf16[2,8,32,512]{3,2,1,0:T(8,128)(2,1)S(1)}, bf16[2,8,32,512]{3,2,1,0:T(8,128)(2,1)}, u32[]{:S(2)}) copy-start(bf16[2,8,32,512]{3,2,1,0:T(8,128)(2,1)} %param.10) | copy-start | bytes 1572868
  3.4 0.9 %copy-start.2 = (bf16[512,256]{1,0:T(8,128)(2,1)S(1)}, bf16[512,256]{1,0:T(8,128)(2,1)}, u32[]{:S(2)}) copy-start(bf16[512,256]{1,0:T(8,128)(2,1)} %wq_hbm.1) | copy-start | bytes 786436
  4.4 0.9 %copy-start.3 = (bf16[512,256]{1,0:T(8,128)(2,1)S(1)}, bf16[512,256]{1,0:T(8,128)(2,1)}, u32[]{:S(2)}) copy-start(bf16[512,256]{1,0:T(8,128)(2,1)} %wk_hbm.1) | copy-start | bytes 786436
  5.3 0.9 %copy-start.4 = (bf16[512,256]{1,0:T(8,128)(2,1)S(1)}, bf16[512,256]{1,0:T(8,128)(2,1)}, u32[]{:S(2)}) copy-start(bf16[512,256]{1,0:T(8,128)(2,1)} %wv_hbm.1) | copy-start | bytes 786436
  6.3 0.9 %copy-start.5 = (bf16[512,256]{1,0:T(8,128)(2,1)S(1)}, bf16[512,256]{1,0:T(8,128)(2,1)}, u32[]{:S(2)}) copy-start(bf16[512,256]{1,0:T(8,128)(2,1)} %wo_hbm.1) | copy-start | bytes 786436
  7.2 0.8 %copy-start.6 = (f32[9,512]{1,0:T(8,128)S(1)}, f32[9,512]{1,0:T(8,128)}, u32[]{:S(2)}) copy-start(f32[9,512]{1,0:T(8,128)} %kern_hbm.1) | copy-start | bytes 55300
